TPU v7x, 512 devices: a whole 4x4x16 slice. The times are simulated.
512 devices in a mesh: dp: 8 (over y, core), seq: 16 (over x, z_lo), mp: 4 (over z_hi).
Axes of the slice: x: 4, y: 4, z: 16 (z_hi: 4, z_lo: 4; z = z_hi * 4 + z_lo), core: 2. Of those that a mesh axis runs over, the one named last changes fastest.
Arguments:
- query: bfloat16 [8, 2560, 1536], P('dp', 'seq'), may hold values from -8 to 8
- key: bfloat16 [8, 2560, 1536], P('dp', 'seq'), may hold values from -8 to 8
- value: bfloat16 [8, 2560, 1536], P('dp', 'seq'), may hold values from -6 to 6
- proj_weight: bfloat16 [1536, 1536], P(None, 'mp'), may hold values from -0.15625 to 0.15625
- grad_out: bfloat16 [8, 2560, 1536], P('dp', 'seq', 'mp'), may hold values from -6 to 6
Outputs:
- attended: bfloat16 [8, 2560, 1536], P('dp', 'seq', 'mp')
- grad_query: bfloat16 [8, 2560, 1536], P('dp', ('seq', 'mp'))
- grad_key: bfloat16 [8, 2560, 1536], P('dp', ('seq', 'mp'))
- grad_value: bfloat16 [8, 2560, 1536], P('dp', ('seq', 'mp'))
- grad_proj: bfloat16 [1536, 1536], P(None, 'mp')
All inputs are finite; a program needn't handle non-finite values.
Results may differ from a plain program's by a relative error of at most 0.012.
Values may be sent and summed in bfloat16 or wider, within the bound.
A program may use at most 64 MiB of HBM per device.

v0:
```python
import math

import jax
import jax.numpy as jnp
from jax import lax
from jax.sharding import PartitionSpec as P

HEADS = 16
HEAD_DIM = 96


def per_device(query, key, value, proj_weight, grad_out):
    frames = query.shape[1]
    model_width = query.shape[2]
    seq_count = lax.axis_size("seq")
    model_count = lax.axis_size("mp")
    piece_rows = frames // model_count
    local_heads = HEADS // seq_count
    gathered_rows = seq_count * piece_rows
    score_scale = 1.0 / math.sqrt(HEAD_DIM)
    piece_index = lax.axis_index("mp")
    head_shape = (model_count, piece_rows, HEADS, HEAD_DIM)

    def own_piece(array):
        return lax.dynamic_slice_in_dim(array, piece_index * piece_rows, piece_rows, 0).reshape(
            piece_rows, HEADS, HEAD_DIM
        )

    keys_local, values_local = (
        lax.all_to_all(own_piece(key[0]), "seq", split_axis=1, concat_axis=0, tiled=True),
        lax.all_to_all(own_piece(value[0]), "seq", split_axis=1, concat_axis=0, tiled=True),
    )
    queries = lax.all_to_all(
        query[0].reshape(head_shape), "seq", split_axis=2, concat_axis=1, tiled=True
    )
    queries = queries.reshape(model_count * gathered_rows, local_heads, HEAD_DIM)
    scores = (
        jnp.einsum("qhd,khd->qhk", queries, keys_local, preferred_element_type=jnp.float32)
        * score_scale
    )
    row_top = lax.pmax(jnp.max(scores, axis=2), "mp")
    unscaled = jnp.exp(scores - row_top[:, :, None])
    weights = unscaled.astype(jnp.bfloat16)
    partial_context = jnp.einsum(
        "qhk,khd->qhd", weights, values_local, preferred_element_type=jnp.float32
    )
    summed, row_total = lax.psum((partial_context, jnp.sum(unscaled, axis=2)), "mp")
    context_wide = summed / row_total[:, :, None]
    context = context_wide.astype(jnp.bfloat16).reshape(
        model_count, gathered_rows, local_heads, HEAD_DIM
    )
    returned = lax.all_to_all(context, "seq", split_axis=1, concat_axis=2, tiled=True)
    flat_context = returned.reshape(frames, model_width)
    attended = jnp.dot(flat_context, proj_weight, preferred_element_type=jnp.float32).astype(
        jnp.bfloat16
    )
    grad_rows = grad_out[0]
    grad_weight = jnp.einsum(
        "fw,fc->wc", flat_context, grad_rows, preferred_element_type=jnp.float32
    )
    grad_proj = lax.psum(grad_weight, ("dp", "seq")).astype(jnp.bfloat16)
    grad_full = lax.psum(
        jnp.einsum("fc,wc->fw", grad_rows, proj_weight, preferred_element_type=jnp.float32), "mp"
    ).astype(jnp.bfloat16)
    grad_context = lax.all_to_all(
        grad_full.reshape(head_shape), "seq", split_axis=2, concat_axis=1, tiled=True
    )
    grad_context = grad_context.reshape(model_count * gathered_rows, local_heads, HEAD_DIM)
    probabilities = unscaled / row_total[:, :, None]
    grad_probs = jnp.einsum(
        "qhd,khd->qhk", grad_context, values_local, preferred_element_type=jnp.float32
    )
    row_delta = jnp.sum(grad_context.astype(jnp.float32) * context_wide, axis=2)
    grad_scores = (probabilities * (grad_probs - row_delta[:, :, None]) * score_scale).astype(
        jnp.bfloat16
    )
    grad_keys = jnp.einsum(
        "qhk,qhd->khd", grad_scores, queries, preferred_element_type=jnp.float32
    ).astype(jnp.bfloat16)
    back_weights = probabilities.astype(jnp.bfloat16)
    grad_values = jnp.einsum(
        "qhk,qhd->khd", back_weights, grad_context, preferred_element_type=jnp.float32
    ).astype(jnp.bfloat16)
    grad_queries = lax.psum_scatter(
        jnp.einsum("qhk,khd->qhd", grad_scores, keys_local, preferred_element_type=jnp.float32),
        "mp",
        scatter_dimension=0,
        tiled=True,
    ).astype(jnp.bfloat16)
    back_query, back_key, back_value = (
        lax.all_to_all(grad_queries, "seq", split_axis=0, concat_axis=1, tiled=True),
        lax.all_to_all(grad_keys, "seq", split_axis=0, concat_axis=1, tiled=True),
        lax.all_to_all(grad_values, "seq", split_axis=0, concat_axis=1, tiled=True),
    )
    return (
        attended[None],
        back_query.reshape(1, piece_rows, model_width),
        back_key.reshape(1, piece_rows, model_width),
        back_value.reshape(1, piece_rows, model_width),
        grad_proj,
    )


def solution(mesh):
    return jax.shard_map(
        per_device,
        mesh=mesh,
        in_specs=(
            P("dp", "seq", None),
            P("dp", "seq", None),
            P("dp", "seq", None),
            P(None, "mp"),
            P("dp", "seq", "mp"),
        ),
        out_specs=(
            P("dp", "seq", "mp"),
            P("dp", ("seq", "mp"), None),
            P("dp", ("seq", "mp"), None),
            P("dp", ("seq", "mp"), None),
            P(None, "mp"),
        ),
        check_vma=False,
    )
```

profile of v0, /device:TPU:128, one launch (start us, length us, event | category | flops | bytes accessed | tf_op | source)
XLA Modules:
  0.0 1116.5 jit_solution(12006535100419278444)
XLA Ops:
  7.2 1.8 reshape_squeeze.3
  9.0 1.0 copy.53
  10.0 8.5 all-to-all-start.2
  18.5 1.0 constant_dynamic-slice_fusion
  20.3 17.5 %all-to-all-done.2 = bf16[4,40,16,96]{3,1,0,2:T(8,128)(2,1)S(1)} async-done(((bf16[4,40,16,96]{3,1,0,2:T(8,128)(2,1)}), bf16[4,40,16,96]{3,1,0,2:T(8,128)(2,1)S(1)}, u32[]{:S(2)}, u32[]{:S(2)}) %all-to-all-start.2) | async-done | bytes 491552 | tf_op jit(solution)/shard_map/all_to_all | solution.py:33
  37.8 4.2 all-to-all-start.1
  42.8 1.4 fusion.28
  44.3 6.2 all-to-all-done.1
  50.5 3.5 all-to-all-start
  54.0 4.7 multiply_reduce_fusion
  58.7 24.0 %pmax.7 = f32[2560]{0:T(1024)S(1)} all-reduce(f32[2560]{0:T(1024)S(1)} %get-tuple-element.9), channel_id=1, replica_groups=mesh['dp'=8,'seq'=16,'mp'=4] {'mp'}, use_global_device_ids=true, to_apply=%region_1.0 | all-reduce | flops 2560 | bytes 20480 | tf_op jit(solution)/shard_map/pmax | solution.py:41
  82.7 4.0 fusion.6
  86.6 65.9 %all-reduce.6 = (f32[2560]{0:T(1024)S(1)}, bf16[160,1536]{1,0:T(8,128)(2,1)}) all-reduce(f32[2560]{0:T(1024)S(1)} %fusion.6, f32[160,1536]{1,0:T(8,128)S(1)} %fusion.28), channel_id=1, replica_groups=mesh['dp'=8,'seq'=16,'mp'=4] {'mp'}, use_global_device_ids=true, to_apply=%region_4.0 | all-reduce | flops 248320 | bytes 1495040 | tf_op jit(solution)/shard_map/psum | solution.py:47
  152.5 1.7 reshape.126
  154.2 1.0 copy.58
  155.2 24.6 %all-to-all-start.4 = ((bf16[4,40,16,96]{3,1,0,2:T(8,128)(2,1)}), bf16[4,40,16,96]{3,1,0,2:T(8,128)(2,1)S(1)}, u32[]{:S(2)}, u32[]{:S(2)}) async-start(bf16[4,40,16,96]{3,1,0,2:T(8,128)(2,1)} %copy.58), calls=%async_computation.4 | async-start | bytes 1310720 | tf_op jit(solution)/shard_map/all_to_all | solution.py:65
  179.9 5.1 convolution_bitcast_fusion.1
  185.1 12.5 %all-to-all-done.4 = bf16[4,40,16,96]{3,1,0,2:T(8,128)(2,1)S(1)} async-done(((bf16[4,40,16,96]{3,1,0,2:T(8,128)(2,1)}), bf16[4,40,16,96]{3,1,0,2:T(8,128)(2,1)S(1)}, u32[]{:S(2)}, u32[]{:S(2)}) %all-to-all-start.4) | async-done | bytes 491552 | tf_op jit(solution)/shard_map/all_to_all | solution.py:65
  197.7 0.9 copy-done.2
  198.6 4.4 fusion.22
  204.3 1.0 reshape.140
  205.3 3.7 all-to-all-start.7
  209.2 1.3 copy.61
  210.5 81.5 %all-reduce.5.cloned.1.call-done = f32[2560,1,96]{0,2,1:T(8,128)} async-done(((f32[2560,1,96]{0,2,1:T(8,128)}), f32[2560,1,96]{0,2,1:T(8,128)}) %all-reduce.5.cloned.1.call-update) | async-done | bytes 983056 | tf_op jit(solution)/shard_map/psum | solution.py:47
  292.0 1.6 multiply_reduce_fusion.1
  293.7 4.3 fusion.4
  298.0 1.7 copy-done.1
  299.6 1.1 fusion.21
  301.5 1.0 reshape.138
  302.5 7.9 all-to-all-start.6
  310.6 1.3 copy.55
  311.9 6.9 all-to-all-done.6
  318.8 3.6 all-to-all-start.3
  322.5 3.7 convolution_bitcast_fusion
  326.5 0.8 reshape.132
  328.5 12.3 %all-to-all-done.3 = bf16[4,640,1,96]{3,0,2,1:T(4,128)(2,1)S(1)} async-done(((bf16[4,640,1,96]{3,0,2,1:T(4,128)(2,1)}), bf16[4,640,1,96]{3,0,2,1:T(4,128)(2,1)S(1)}, u32[]{:S(2)}, u32[]{:S(2)}) %all-to-all-start.3) | async-done | bytes 491552 | tf_op jit(solution)/shard_map/all_to_all | solution.py:52
  341.0 1.5 reshape.125
  342.5 1.7 fusion.26
  344.2 36.8 %reduce-scatter.2.cloned.1.call-done = f32[640,1,96]{0,2,1:T(8,128)} async-done(((f32[2560,1,96]{0,2,1:T(8,128)}), f32[640,1,96]{0,2,1:T(8,128)}) %reduce-scatter.2.cloned.1.call-update) | async-done | bytes 245776 | tf_op jit(solution)/shard_map/reduce_scatter | solution.py:84
  380.9 1.6 convert_element_type.70
  382.6 2.2 reduce.6
  384.7 1.7 copy.71
  386.4 1.9 reshape.136
  388.3 4.6 all-to-all-start.5
  392.9 711.9 %all-reduce.7 = bf16[1536,384]{1,0:T(8,128)(2,1)} all-reduce(f32[1536,384]{1,0:T(8,128)S(1)} %fusion.26), channel_id=1, replica_groups=mesh['dp'=8,'seq'=16,'mp'=4] {'dp','seq'}, use_global_device_ids=true, to_apply=%region_8.0 | all-reduce | flops 589824 | bytes 3538944 | tf_op jit(solution)/shard_map/psum | solution.py:61
  1104.9 2.1 fusion.20
  1107.0 1.8 reshape.137
  1108.9 0.8 reshape.129
  (36 shorter events, 6.0 us)
Async XLA Ops:
  7.2 35.7 %copy-start = (bf16[1536,384]{1,0:T(8,128)(2,1)S(1)}, bf16[1536,384]{1,0:T(8,128)(2,1)}, u32[]{:S(2)}) copy-start(bf16[1536,384]{1,0:T(8,128)(2,1)} %param.8) | copy-start | bytes 3538948
  10.0 27.8 %all-to-all-start.2 = ((bf16[4,40,16,96]{3,1,0,2:T(8,128)(2,1)}), bf16[4,40,16,96]{3,1,0,2:T(8,128)(2,1)S(1)}, u32[]{:S(2)}, u32[]{:S(2)}) async-start(bf16[4,40,16,96]{3,1,0,2:T(8,128)(2,1)} %copy.53), calls=%async_computation.2 | async-start | bytes 1310720 | tf_op jit(solution)/shard_map/all_to_all | solution.py:33
  37.8 12.7 %all-to-all-start.1 = ((bf16[40,16,96]{2,0,1:T(8,128)(2,1)}), bf16[40,16,96]{2,0,1:T(8,128)(2,1)}, u32[]{:S(2)}, u32[]{:S(2)}) async-start(bf16[40,16,96]{2,0,1:T(8,128)(2,1)} %copy.52), calls=%async_computation.1 | async-start | bytes 327680 | tf_op jit(solution)/shard_map/all_to_all | solution.py:30
  50.5 104.7 %all-to-all-start = ((bf16[40,16,96]{2,0,1:T(8,128)(2,1)}), bf16[40,16,96]{2,0,1:T(8,128)(2,1)S(1)}, u32[]{:S(2)}, u32[]{:S(2)}) async-start(bf16[40,16,96]{2,0,1:T(8,128)(2,1)} %copy.51), calls=%async_computation | async-start | bytes 327680 | tf_op jit(solution)/shard_map/all_to_all | solution.py:31
  155.2 42.4 %all-to-all-start.4 = ((bf16[4,40,16,96]{3,1,0,2:T(8,128)(2,1)}), bf16[4,40,16,96]{3,1,0,2:T(8,128)(2,1)S(1)}, u32[]{:S(2)}, u32[]{:S(2)}) async-start(bf16[4,40,16,96]{3,1,0,2:T(8,128)(2,1)} %copy.58), calls=%async_computation.4 | async-start | bytes 1310720 | tf_op jit(solution)/shard_map/all_to_all | solution.py:65
  179.9 112.1 %all-reduce.5.cloned.1.call-start = ((), (), s32[]{:S(2)}) async-start(), calls=%async_computation.9 | async-start | bytes 1966080 | tf_op jit(solution)/shard_map/psum | solution.py:47
  197.7 0.9 copy-start.2
  205.3 97.2 %all-to-all-start.7 = ((bf16[16,2,1920]{2,1,0:T(2,128)(2,1)}), bf16[16,2,1920]{2,1,0:T(2,128)(2,1)S(1)}, u32[]{:S(2)}, u32[]{:S(2)}) async-start(bf16[16,2,1920]{2,1,0:T(2,128)(2,1)} %reshape.140), calls=%async_computation.8 | async-start | bytes 245760 | tf_op jit(solution)/shard_map/all_to_all | solution.py:93
  297.9 1.7 copy-start.1
  302.5 16.3 %all-to-all-start.6 = ((bf16[16,2,1920]{2,1,0:T(2,128)(2,1)}), bf16[16,2,1920]{2,1,0:T(2,128)(2,1)S(1)}, u32[]{:S(2)}, u32[]{:S(2)}) async-start(bf16[16,2,1920]{2,1,0:T(2,128)(2,1)} %reshape.138), calls=%async_computation.7 | async-start | bytes 245760 | tf_op jit(solution)/shard_map/all_to_all | solution.py:92
  318.8 22.0 %all-to-all-start.3 = ((bf16[4,640,1,96]{3,0,2,1:T(4,128)(2,1)}), bf16[4,640,1,96]{3,0,2,1:T(4,128)(2,1)S(1)}, u32[]{:S(2)}, u32[]{:S(2)}) async-start(bf16[4,640,1,96]{3,0,2,1:T(4,128)(2,1)} %copy.55), calls=%async_computation.3 | async-start | bytes 1310720 | tf_op jit(solution)/shard_map/all_to_all | solution.py:52
  322.4 58.5 %reduce-scatter.2.cloned.1.call-start = ((), (), s32[]{:S(2)}) async-start(), calls=%async_computation.10 | async-start | bytes 1228800 | tf_op jit(solution)/shard_map/reduce_scatter | solution.py:84
  388.3 718.7 %all-to-all-start.5 = ((bf16[16,2,1920]{2,1,0:T(2,128)(2,1)}), bf16[16,2,1920]{2,1,0:T(2,128)(2,1)}, u32[]{:S(2)}, u32[]{:S(2)}) async-start(bf16[16,2,1920]{2,1,0:T(2,128)(2,1)} %reshape.136), calls=%async_computation.6 | async-start | bytes 245760 | tf_op jit(solution)/shard_map/all_to_all | solution.py:91
Sparse Core Ops, SparseCore 0:
  185.2 106.7 all-reduce.4
  326.9 53.9 reduce-scatter.1
where the time goes:
time: 1120 us
  blocking collectives  802 us (72%)
  waiting for transfers between devices  174 us (16%)
  starting transfers between devices  60.7 us (5%)
  matrix products  28.5 us (3%)
  local copies, waits for them, and re-layouts  26.8 us (2%)
  between operations  14.3 us (1%)
    psum x1, blocking collectives, per_device(): grad_proj = lax.psum(grad_weight, ('dp', 'seq')).astype(jnp.bfloat16)  712 us
    psum x1, waiting for transfers between devices, per_device(): lax.psum((partial_context, jnp.sum(unscaled, axis=2)), 'mp')  81.5 us
    psum x1, blocking collectives, per_device(): lax.psum((partial_context, jnp.sum(unscaled, axis=2)), 'mp')  65.9 us
    reduce_scatter x1, waiting for transfers between devices, per_device(): lax.psum_scatter(jnp.einsum('qhk,khd->qhd', grad_scores, keys_local, pref...  36.8 us
    all_to_all x1, starting transfers between devices, per_device(): lax.all_to_all(grad_full.reshape(head_shape), 'seq', split_axis=2, concat...  24.6 us
    pmax x1, blocking collectives, per_device(): row_top = lax.pmax(jnp.max(scores, axis=2), 'mp')  24 us
  transfers between devices with their start and end apart: 10, of which 7 were waited for; matrix products, arithmetic and copies ran while one was open for 5% of the time, Pallas kernels for 0%

commit v1 on v0

v1 whole, which is shorter than its diff:
```python
import math

import jax
import jax.numpy as jnp
from jax import lax
from jax.experimental import pallas as pl
from jax.experimental.pallas import tpu as pltpu
from jax.sharding import PartitionSpec as P

MESH = pl.DeviceIdType.MESH
F32 = jnp.float32
BF16 = jnp.bfloat16
HD = 96
SCALE = 1.0 / math.sqrt(HD)
EXP2_SCALE = SCALE * math.log2(math.e)
NT = (((1,), (1,)), ((), ()))
NN = (((1,), (0,)), ((), ()))
TN = (((0,), (0,)), ((), ()))
FR = 160
QN = 640
CW = 384


def dot(a, b, dims):
    return lax.dot_general(a, b, dims, preferred_element_type=F32)


def copy_to(src, dst, send, recv, device):
    return pltpu.make_async_remote_copy(
        src_ref=src, dst_ref=dst, send_sem=send, recv_sem=recv, device_id=device, device_id_type=MESH
    )


def kernel(
    q_ref, k_ref, v_ref, w_ref, go_ref,
    att_ref, gq_ref, gk_ref, gv_ref, gp_ref,
    zsq, zskv, qbuf, kvbuf, gcs, gcr, gall, scores, ctxt, ctxs, ctxr, dqt, dqf, rss, rsr, own_kv,
    gqs, gqr, gks, gkr, att_acc, gps, gpr, gpo, gsum, xst, xrt, zst, gpf,
    zq_s, zq_r, zkv_s, zkv_r, xkv_s, xkv_r, gc_s, gc_r, ctx_s, ctx_r, rs_s, rs_r,
    gq_s, gq_r, gk_s, gk_r, gp_s, gp_r, px_s, px_r, pz_s, pz_r, ax_s, ax_r, ad_s, ad_r,
):
    d = lax.axis_index("dp")
    s = lax.axis_index("seq")
    m = lax.axis_index("mp")
    x = s // 4
    zl = s % 4
    z = m * 4 + zl
    core = d % 2

    def zdev(zz):
        return {"seq": x * 4 + zz % 4, "mp": zz // 4}

    def xdev(xx):
        return {"seq": xx * 4 + zl}

    def ddev(dd):
        return {"dp": dd}

    barrier = pltpu.get_barrier_semaphore()
    for k in range(1, 16):
        pl.semaphore_signal(barrier, inc=1, device_id=zdev((z + k) % 16), device_id_type=MESH)
    for k in range(1, 4):
        pl.semaphore_signal(barrier, inc=1, device_id=xdev((x + k) % 4), device_id_type=MESH)
    for k in range(1, 8):
        pl.semaphore_signal(barrier, inc=1, device_id=ddev((d + k) % 8), device_id_type=MESH)

    def offset(j):
        return (0, 1, 2 - 4 * core, -1)[j]

    def head_of(j):
        return (z + offset(j) + 16) % 16

    rows = lax.broadcasted_iota(jnp.int32, (CW, HD), 0)
    cols = lax.broadcasted_iota(jnp.int32, (CW, HD), 1)
    for j in (1, 3, 2, 0):
        h = head_of(j)
        pick = jnp.where(rows - cols == HD * (h % 4), 1.0, 0.0).astype(BF16)
        window = pl.ds(pl.multiple_of(CW * (h // 4), 128), CW)
        kh = dot(k_ref[:, window], pick, NN).astype(BF16)
        vh = dot(v_ref[:, window], pick, NN).astype(BF16)
        qh = dot(q_ref[:, window], pick, NN).astype(BF16)
        if j == 0:
            kvbuf[0, 0] = kh
            kvbuf[0, 1] = vh
            qbuf[0:FR, :] = qh
        else:
            zskv[j, 0] = kh
            zskv[j, 1] = vh
            zsq[j] = qh

    pl.semaphore_wait(barrier, 25)

    def zkv_copy(j):
        return copy_to(zskv.at[j], kvbuf.at[j], zkv_s.at[j], zkv_r.at[j], zdev(head_of(j)))

    def zq_copy(j):
        return copy_to(zsq.at[j], qbuf.at[pl.ds(FR * j, FR)], zq_s.at[j], zq_r.at[j], zdev(head_of(j)))

    def xkv_copy(xo, j):
        slot = xo * 4 + j
        return copy_to(kvbuf.at[j], kvbuf.at[slot], xkv_s.at[slot], xkv_r.at[slot], xdev((x + xo) % 4))

    for j in (1, 3, 2):
        zkv_copy(j).start()
    for xo in (2, 1, 3):
        xkv_copy(xo, 0).start()
    for j in (1, 3, 2):
        zq_copy(j).start()

    def gc_copy(k):
        return copy_to(gcs.at[k], gcr.at[k], gc_s.at[k], gc_r.at[k], zdev((z + k) % 16))

    def gc_step(k):
        h = (z + k) % 16
        part = dot(go_ref[...], w_ref[pl.ds(pl.multiple_of(HD * h, 32), HD), :], NT)
        gcs[k] = part.astype(BF16)
        gc_copy(k).start()

    def forward_x(j):
        zkv_copy(j).wait_recv()
        for xo in (2, 1, 3):
            xkv_copy(xo, j).start()

    order = (8, 7, 9, 6, 10, 5, 11, 4, 12, 3, 13, 2, 14, 1, 15)
    for k in order[:5]:
        gc_step(k)
    forward_x(1)
    forward_x(3)
    for k in order[5:10]:
        gc_step(k)
    forward_x(2)
    for k in order[10:]:
        gc_step(k)
    gcs[0] = dot(go_ref[...], w_ref[pl.ds(pl.multiple_of(HD * z, 32), HD), :], NT).astype(BF16)

    for j in (1, 3, 2):
        zq_copy(j).wait_recv()

    def score_slot(slot, top):
        block = dot(kvbuf[slot, 0], qbuf[...], NT)
        scores[slot] = block
        return jnp.maximum(top, jnp.max(block.reshape(FR // 8, 8, QN), axis=0))

    top = jnp.full((8, QN), -jnp.inf, F32)
    top = lax.fori_loop(0, 4, score_slot, top)
    for xo in (1, 3, 2):
        for j in (0, 1, 3, 2):
            xkv_copy(xo, j).wait_recv()
            top = score_slot(xo * 4 + j, top)
    row_top = jnp.max(top, axis=0, keepdims=True)

    ctxt[...] = jnp.zeros_like(ctxt)

    def soft_slot(slot, total):
        p = jnp.exp2((scores[slot] - row_top) * EXP2_SCALE)
        scores[slot] = p
        ctxt[...] += dot(kvbuf[slot, 1], p.astype(BF16), TN)
        return total + jnp.sum(p.reshape(FR // 8, 8, QN), axis=0)

    total = lax.fori_loop(0, 16, soft_slot, jnp.zeros((8, QN), F32))
    inverse = 1.0 / jnp.sum(total, axis=0, keepdims=True)
    wide = ctxt[...] * inverse
    ctxt[...] = wide
    narrow = wide.T.astype(BF16)
    for j in range(4):
        ctxs[j] = narrow[j * FR : (j + 1) * FR, :]

    def ctx_copy(k):
        return copy_to(ctxs.at[k % 4], ctxr.at[k], ctx_s.at[k], ctx_r.at[k], zdev((z - k + 16) % 16))

    for k in order:
        ctx_copy(k).start()
    ctxr[0] = ctxs[0]

    for j in range(4):
        acc = None
        for i in range(4):
            k = j + 4 * i
            if k == 0:
                part = gcs[0]
            else:
                gc_copy(k).wait_recv()
                part = gcr[k]
            part = part.astype(F32)
            acc = part if acc is None else acc + part
        gall[j * FR : (j + 1) * FR, :] = acc.astype(BF16)
    delta = jnp.sum(gall[...].astype(F32).T * ctxt[...], axis=0, keepdims=True)

    dqt[...] = jnp.zeros_like(dqt)

    def back_slot(slot):
        p = scores[slot] * inverse
        gprob = dot(kvbuf[slot, 1], gall[...], NT)
        ds = (p * (gprob - delta) * SCALE).astype(BF16)
        dk = dot(ds, qbuf[...], NN)
        dv = dot(p.astype(BF16), gall[...], NN)
        dqt[...] += dot(kvbuf[slot, 0], ds, TN)
        return dk, dv

    def rs_copy(slot):
        xo = slot // 4
        return copy_to(rss.at[slot], rsr.at[slot], rs_s.at[slot], rs_r.at[slot], xdev((x - xo + 4) % 4))

    def away_slot(i, carry):
        slot = 15 - i
        dk, dv = back_slot(slot)
        rss[slot, 0] = dk.astype(BF16)
        rss[slot, 1] = dv.astype(BF16)
        rs_copy(slot).start()
        return carry

    lax.fori_loop(0, 12, away_slot, 0)

    def own_slot(slot, carry):
        dk, dv = back_slot(slot)
        own_kv[slot, 0] = dk
        own_kv[slot, 1] = dv
        return carry

    lax.fori_loop(0, 4, own_slot, 0)

    dqf[...] = dqt[...].T

    def gq_copy(k):
        return copy_to(gqs.at[k], gqr.at[k], gq_s.at[k], gq_r.at[k], zdev((z - k + 16) % 16))

    def gk_copy(k):
        return copy_to(gks.at[k], gkr.at[k], gk_s.at[k], gk_r.at[k], zdev((z - k + 16) % 16))

    def piece_start(k):
        return pl.multiple_of(40 * (((z - k + 16) % 16) // 4), 8)

    pad = jnp.zeros((8, HD), F32)
    for k in order:
        part = dqf[pl.ds(FR * (k % 4) + piece_start(k), 40), :]
        gqs[k] = jnp.concatenate([part, pad], axis=0).astype(BF16)
        gq_copy(k).start()
    gqr[0] = jnp.concatenate([dqf[pl.ds(piece_start(0), 40), :], pad], axis=0).astype(BF16)

    for j in range(4):
        for xo in (3, 2, 1):
            rs_copy(xo * 4 + j).wait_recv()
        for t in range(2):
            own_kv[j, t] = (
                own_kv[j, t]
                + rsr[4 + j, t].astype(F32)
                + rsr[8 + j, t].astype(F32)
                + rsr[12 + j, t].astype(F32)
            )

    def gk_piece(k):
        start = piece_start(k)
        return jnp.concatenate(
            [own_kv[k % 4, 0, pl.ds(start, 40), :], own_kv[k % 4, 1, pl.ds(start, 40), :]], axis=0
        ).astype(BF16)

    for k in order:
        gks[k] = gk_piece(k)
        gk_copy(k).start()
    gkr[0] = gk_piece(0)

    att_acc[...] = jnp.zeros_like(att_acc)

    def owner(k):
        h = (z + k) % 16
        return h // 2, h % 2

    def gp_copy(k):
        dd, hh = owner(k)
        e = (dd - d + 8) % 8
        return copy_to(gps.at[k], gpr.at[e, hh], gp_s.at[k], gp_r.at[e, hh], ddev(dd))

    for k in (0,) + order[::-1]:
        if k > 0:
            ctx_copy(k).wait_recv()
        h = (z + k) % 16
        dd, hh = owner(k)
        att_acc[...] += dot(ctxr[k], w_ref[pl.ds(pl.multiple_of(HD * h, 32), HD), :], NN)
        part = dot(ctxr[k], go_ref[...], TN)

        @pl.when(dd == d)
        def _():
            gpo[hh] = part

        @pl.when(dd != d)
        def _():
            gps[k] = part.astype(BF16)
            gp_copy(k).start()

    att_ref[...] = att_acc[...].astype(BF16)

    for hh in range(2):
        for e in range(1, 8):
            copy_to(gps.at[0], gpr.at[e, hh], gp_s.at[0], gp_r.at[e, hh], ddev((d + e) % 8)).wait_recv()
        acc = gpo[hh]
        for e in range(1, 8):
            acc = acc + gpr[e, hh].astype(F32)
        gsum[hh] = acc

    def px_copy(xo):
        return copy_to(xst.at[xo], xrt.at[xo], px_s.at[xo], px_r.at[xo], xdev((x + xo) % 4))

    def quarter(xx):
        return gsum[xx // 2, pl.ds(pl.multiple_of(48 * (xx % 2), 16), 48), :]

    for xo in (2, 1, 3):
        xst[xo] = quarter((x + xo) % 4).astype(BF16)
        px_copy(xo).start()
    acc = quarter(x)
    for xo in (1, 3, 2):
        px_copy(xo).wait_recv()
        acc = acc + xrt[xo].astype(F32)
    zst[zl] = acc.astype(BF16)

    def pz_copy(o, source):
        return copy_to(
            zst.at[zl], zst.at[source], pz_s.at[o], pz_r.at[o], {"seq": x * 4 + (zl + o) % 4}
        )

    for o in (2, 1, 3):
        pz_copy(o, zl).start()
    for o in (1, 3, 2):
        pz_copy(o, (zl - o + 4) % 4).wait_recv()
    acc = zst[0].astype(F32)
    for i in range(1, 4):
        acc = acc + zst[i].astype(F32)
    gpf[d, x] = acc.astype(BF16)

    def ax_copy(xo, source):
        return copy_to(gpf.at[d, x], gpf.at[d, source], ax_s.at[xo], ax_r.at[xo], xdev((x + xo) % 4))

    def ad_copy(e, source):
        return copy_to(gpf.at[d], gpf.at[source], ad_s.at[e], ad_r.at[e], ddev((d + e) % 8))

    for xo in (2, 1, 3):
        ax_copy(xo, x).start()
    for xo in (1, 3, 2):
        ax_copy(xo, (x - xo + 4) % 4).wait_recv()
    for e in range(1, 8):
        ad_copy(e, d).start()

    for k in order:
        gq_copy(k).wait_recv()
        gk_copy(k).wait_recv()
    for group in range(4):
        lanes = pl.ds(CW * group, CW)
        slots = [(4 * group + i - z + 16) % 16 for i in range(4)]
        gq_ref[:, lanes] = jnp.concatenate([gqr[t, 0:40, :] for t in slots], axis=1)
        gk_ref[:, lanes] = jnp.concatenate([gkr[t, 0:40, :] for t in slots], axis=1)
        gv_ref[:, lanes] = jnp.concatenate([gkr[t, 40:80, :] for t in slots], axis=1)

    for e in range(1, 8):
        ad_copy(e, (d - e + 8) % 8).wait_recv()
    for i in range(8):
        for t in range(4):
            gp_ref[192 * i + 48 * t : 192 * i + 48 * (t + 1), :] = gpf[i, t]

    for j in range(1, 4):
        zkv_copy(j).wait_send()
        zq_copy(j).wait_send()
        px_copy(j).wait_send()
        pz_copy(j, zl).wait_send()
        ax_copy(j, x).wait_send()
    for xo in range(1, 4):
        for j in range(4):
            xkv_copy(xo, j).wait_send()
            rs_copy(xo * 4 + j).wait_send()
    for k in range(1, 16):
        gc_copy(k).wait_send()
        ctx_copy(k).wait_send()
        gq_copy(k).wait_send()
        gk_copy(k).wait_send()
    for k in range(16):

        @pl.when(owner(k)[0] != d)
        def _():
            gp_copy(k).wait_send()

    for e in range(1, 8):
        ad_copy(e, d).wait_send()


def per_device(query, key, value, proj_weight, grad_out):
    vmem = pl.BlockSpec(memory_space=pltpu.VMEM)
    dma = pltpu.SemaphoreType.DMA
    width = query.shape[2]
    outs = pl.pallas_call(
        kernel,
        out_shape=(
            jax.ShapeDtypeStruct((FR, CW), BF16),
            jax.ShapeDtypeStruct((40, width), BF16),
            jax.ShapeDtypeStruct((40, width), BF16),
            jax.ShapeDtypeStruct((40, width), BF16),
            jax.ShapeDtypeStruct((width, CW), BF16),
        ),
        in_specs=[vmem] * 5,
        out_specs=(vmem,) * 5,
        scratch_shapes=[
            pltpu.VMEM((4, FR, HD), BF16),
            pltpu.VMEM((4, 2, FR, HD), BF16),
            pltpu.VMEM((QN, HD), BF16),
            pltpu.VMEM((16, 2, FR, HD), BF16),
            pltpu.VMEM((16, FR, HD), BF16),
            pltpu.VMEM((16, FR, HD), BF16),
            pltpu.VMEM((QN, HD), BF16),
            pltpu.VMEM((16, FR, QN), F32),
            pltpu.VMEM((HD, QN), F32),
            pltpu.VMEM((4, FR, HD), BF16),
            pltpu.VMEM((16, FR, HD), BF16),
            pltpu.VMEM((HD, QN), F32),
            pltpu.VMEM((QN, HD), F32),
            pltpu.VMEM((16, 2, FR, HD), BF16),
            pltpu.VMEM((16, 2, FR, HD), BF16),
            pltpu.VMEM((4, 2, FR, HD), F32),
            pltpu.VMEM((16, 48, HD), BF16),
            pltpu.VMEM((16, 48, HD), BF16),
            pltpu.VMEM((16, 80, HD), BF16),
            pltpu.VMEM((16, 80, HD), BF16),
            pltpu.VMEM((FR, CW), F32),
            pltpu.VMEM((16, HD, CW), BF16),
            pltpu.VMEM((8, 2, HD, CW), BF16),
            pltpu.VMEM((2, HD, CW), F32),
            pltpu.VMEM((2, HD, CW), F32),
            pltpu.VMEM((4, 48, CW), BF16),
            pltpu.VMEM((4, 48, CW), BF16),
            pltpu.VMEM((4, 48, CW), BF16),
            pltpu.VMEM((8, 4, 48, CW), BF16),
            dma((4,)), dma((4,)),
            dma((4,)), dma((4,)),
            dma((16,)), dma((16,)),
            dma((16,)), dma((16,)),
            dma((16,)), dma((16,)),
            dma((16,)), dma((16,)),
            dma((16,)), dma((16,)),
            dma((16,)), dma((16,)),
            dma((16,)), dma((8, 2)),
            dma((4,)), dma((4,)),
            dma((4,)), dma((4,)),
            dma((4,)), dma((4,)),
            dma((8,)), dma((8,)),
        ],
        compiler_params=pltpu.CompilerParams(
            collective_id=0, has_side_effects=True, vmem_limit_bytes=48 * 1024 * 1024
        ),
        name="attention",
    )(query[0], key[0], value[0], proj_weight, grad_out[0])
    att, gq, gk, gv, gp = outs
    return att[None], gq[None], gk[None], gv[None], gp


def solution(mesh):
    return jax.shard_map(
        per_device,
        mesh=mesh,
        in_specs=(
            P("dp", "seq", None),
            P("dp", "seq", None),
            P("dp", "seq", None),
            P(None, "mp"),
            P("dp", "seq", "mp"),
        ),
        out_specs=(
            P("dp", "seq", "mp"),
            P("dp", ("seq", "mp"), None),
            P("dp", ("seq", "mp"), None),
            P("dp", ("seq", "mp"), None),
            P(None, "mp"),
        ),
        check_vma=False,
    )
```

time: 1120 us -> 141 us (0.13)
  the two profiles are of different devices: /device:TPU:128 before, /device:TPU:1 now
where the time goes in v1:
time: 141 us
  Pallas kernels  131 us (93%)
  local copies, waits for them, and re-layouts  8.86 us (6%)
    pallas_call x1, Pallas kernels, per_device(): pl.pallas_call(kernel, out_shape=(jax.ShapeDtypeStruct((FR, CW), BF16), j...  131 us
    unnamed x15, local copies, waits for them, and re-layouts  8.86 us

profile of v1, /device:TPU:1, one launch (start us, length us, event | category | flops | bytes accessed | tf_op | source)
XLA Modules:
  0.0 140.6 jit_solution(4675602990299202127)
XLA Ops:
  0.6 0.0 copy-start
  0.6 1.3 copy-done
  1.9 0.0 copy-start.1
  1.9 1.0 copy-done.1
  2.9 0.0 copy-start.2
  2.9 1.0 copy-done.2
  4.0 0.0 copy-start.3
  4.0 1.0 copy-done.3
  5.0 0.0 copy-start.4
  5.0 0.9 copy-done.4
  5.9 131.0 %attention.1 = (bf16[160,384]{1,0:T(8,128)(2,1)S(1)}, bf16[40,1536]{1,0:T(8,128)(2,1)S(1)}, bf16[40,1536]{1,0:T(8,128)(2,1)S(1)}, bf16[40,1536]{1,0:T(8,128)(2,1)S(1)}, bf16[1536,384]{1,0:T(8,128)(2,1)S(1)}) custom-call(bf16[160,1536]{1,0:T(8,128)(2,1)S(1)} %bitcast.8, bf16[160,1536]{1,0:T(8,128)(2,1)S(1)} %bitcast.9, bf16[160,1536]{1,0:T(8,128)(2,1)S(1)} %bitcast.10, ...), custom_call_target="tpu_custom_call" | custom-call | tf_op jit(solution)/shard_map/attention/pallas_call | solution.py:387
  136.9 0.7 copy.15
  137.6 0.6 copy.16
  138.2 0.6 copy.17
  138.9 0.6 copy.18
  139.5 1.0 copy.19
Async XLA Ops:
  0.6 1.3 copy-start
  1.9 1.0 copy-start.1
  2.9 1.0 copy-start.2
  4.0 1.0 copy-start.3
  5.0 0.9 copy-start.4

commit v2 on v1

v2 whole, which is shorter than its diff:
```python
import math

import jax
import jax.numpy as jnp
from jax import lax
from jax.experimental import pallas as pl
from jax.experimental.pallas import tpu as pltpu
from jax.sharding import PartitionSpec as P

MESH = pl.DeviceIdType.MESH
F32 = jnp.float32
BF16 = jnp.bfloat16
HD = 96
SCALE = 1.0 / math.sqrt(HD)
EXP2_SCALE = SCALE * math.log2(math.e)
NT = (((1,), (1,)), ((), ()))
NN = (((1,), (0,)), ((), ()))
TN = (((0,), (0,)), ((), ()))
FR = 160
QN = 640
CW = 384


def dot(a, b, dims):
    return lax.dot_general(a, b, dims, preferred_element_type=F32)


def pack(block):
    t = block.shape[0] // 5
    tail = block[4 * t :, :]
    side = jnp.concatenate(
        [tail[:, 0:32], tail[:, 32:64], tail[:, 64:96], jnp.zeros((t, 32), block.dtype)], axis=0
    )
    return jnp.concatenate([block[: 4 * t, :], side], axis=1)


def unpack(block):
    t = block.shape[0] // 4
    side = block[:, 96:128]
    tail = jnp.concatenate([side[0:t], side[t : 2 * t], side[2 * t : 3 * t]], axis=1)
    return jnp.concatenate([block[:, 0:96], tail], axis=0)


def pack_pair(a, b):
    low = jnp.concatenate([b[0:80, 32:96], b[80:160, 32:96]], axis=1)
    return jnp.concatenate([jnp.concatenate([a, b[:, 0:32]], axis=1), low], axis=0)


def unpack_pair(block):
    low = jnp.concatenate([block[160:240, 0:64], block[160:240, 64:128]], axis=0)
    return block[0:160, 0:96], jnp.concatenate([block[0:160, 96:128], low], axis=1)


def copy_to(src, dst, send, recv, device):
    return pltpu.make_async_remote_copy(
        src_ref=src, dst_ref=dst, send_sem=send, recv_sem=recv, device_id=device, device_id_type=MESH
    )


def kernel(
    q_hbm, k_hbm, v_hbm, w_hbm, go_hbm,
    att_ref, gq_ref, gk_ref, gv_ref, gp_ref,
    q_ref, k_ref, v_ref, w_ref, go_ref,
    zsq, zskv, qin, qbuf, kvbuf, vbuf, gcs, gcr, gall, scores, tops, ctxt, ctxs, ctxr, dqt, dqf, rss, rsr, own_kv, gk_all, gv_all,
    gqs, gqr, gks, gkr, att_acc, gps, gpr, gpo, gsum, gsb, prr, gpf,
    zq_s, zq_r, zkv_s, zkv_r, xkv_s, xkv_r, gc_s, gc_r, ctx_s, ctx_r, rs_s, rs_r,
    gq_s, gq_r, gk_s, gk_r, gp_s, gp_r, ps_s, ps_r, as_s, as_r, ad_s, ad_r, ac_s, ac_r, in_s,
):
    d = lax.axis_index("dp")
    s = lax.axis_index("seq")
    m = lax.axis_index("mp")
    x = s // 4
    zl = s % 4
    z = m * 4 + zl
    core = d % 2

    def zdev(zz):
        return {"seq": x * 4 + zz % 4, "mp": zz // 4}

    def xdev(xx):
        return {"seq": xx * 4 + zl}

    def ddev(dd):
        return {"dp": dd}

    barrier = pltpu.get_barrier_semaphore()
    for k in range(1, 16):
        pl.semaphore_signal(barrier, inc=1, device_id=zdev((z + k) % 16), device_id_type=MESH)
    for k in range(1, 4):
        for i in range(4):
            row = {"seq": (x + k) % 4 * 4 + (zl + i) % 4}
            pl.semaphore_signal(barrier, inc=1, device_id=row, device_id_type=MESH)
    for k in range(1, 8):
        pl.semaphore_signal(barrier, inc=1, device_id=ddev((d + k) % 8), device_id_type=MESH)

    fetches = [
        pltpu.make_async_copy(src, dst, in_s.at[i])
        for i, (src, dst) in enumerate(
            ((k_hbm, k_ref), (v_hbm, v_ref), (q_hbm, q_ref), (w_hbm, w_ref), (go_hbm, go_ref))
        )
    ]
    for fetch in fetches:
        fetch.start()

    def offset(j):
        return (0, 1, 2 - 4 * core, -1)[j]

    def head_of(j):
        return (z + offset(j) + 16) % 16

    rows = lax.broadcasted_iota(jnp.int32, (CW, HD), 0)
    cols = lax.broadcasted_iota(jnp.int32, (CW, HD), 1)
    wide_rows = lax.broadcasted_iota(jnp.int32, (CW, 128), 0)
    wide_cols = lax.broadcasted_iota(jnp.int32, (CW, 128), 1)

    def wide_pick(start, lane, count):
        inside = (wide_cols >= lane) & (wide_cols < lane + count)
        return jnp.where((wide_rows - start == wide_cols - lane) & inside, 1.0, 0.0).astype(BF16)

    def window(h):
        return pl.ds(pl.multiple_of(CW * (h // 4), 128), CW)

    fetches[0].wait()
    fetches[1].wait()
    for j in (1, 3, 2, 0):
        h = head_of(j)
        start = HD * (h % 4)
        kh = k_ref[:, window(h)]
        vh = v_ref[:, window(h)]
        top_part = dot(kh, wide_pick(start, 0, 96), NN) + dot(vh, wide_pick(start, 96, 32), NN)
        low_part = dot(vh[0:80], wide_pick(start + 32, 0, 64), NN) + dot(
            vh[80:160], wide_pick(start + 32, 64, 64), NN
        )
        if j == 0:
            kvbuf[0, 0:160, :] = top_part.astype(BF16)
            kvbuf[0, 160:240, :] = low_part.astype(BF16)
        else:
            zskv[j, 0:160, :] = top_part.astype(BF16)
            zskv[j, 160:240, :] = low_part.astype(BF16)

    pl.semaphore_wait(barrier, 34)

    def zkv_copy(j):
        return copy_to(zskv.at[j], kvbuf.at[j], zkv_s.at[j], zkv_r.at[j], zdev(head_of(j)))

    def zq_copy(j):
        return copy_to(zsq.at[j], qin.at[j], zq_s.at[j], zq_r.at[j], zdev(head_of(j)))

    def xkv_copy(xo, j):
        slot = xo * 4 + j
        return copy_to(kvbuf.at[j], kvbuf.at[slot], xkv_s.at[slot], xkv_r.at[slot], xdev((x + xo) % 4))

    for j in (1, 3, 2):
        zkv_copy(j).start()
    for xo in (2, 1, 3):
        xkv_copy(xo, 0).start()
    fetches[2].wait()
    for j in (1, 3, 2, 0):
        h = head_of(j)
        pick = jnp.where(rows - cols == HD * (h % 4), 1.0, 0.0).astype(BF16)
        qh = dot(q_ref[:, window(h)], pick, NN)
        if j == 0:
            qbuf[0:FR, :] = qh.astype(BF16)
        else:
            zsq[j] = pack(qh).astype(BF16)
            zq_copy(j).start()
    fetches[3].wait()
    fetches[4].wait()

    def gc_copy(k):
        return copy_to(gcs.at[k], gcr.at[k], gc_s.at[k], gc_r.at[k], zdev((z + k) % 16))

    def gc_step(k):
        h = (z + k) % 16
        part = dot(go_ref[...], w_ref[pl.ds(pl.multiple_of(HD * h, 32), HD), :], NT)
        gcs[k] = pack(part).astype(BF16)

    order = (8, 7, 9, 6, 10, 5, 11, 4, 12, 3, 13, 2, 14, 1, 15)
    for k in order:
        gc_step(k)
    for j in (1, 3, 2):
        zkv_copy(j).wait_recv()
        for xo in (2, 1, 3):
            xkv_copy(xo, j).start()
    for k in order:
        gc_copy(k).start()
    gcs[0] = pack(dot(go_ref[...], w_ref[pl.ds(pl.multiple_of(HD * z, 32), HD), :], NT)).astype(BF16)

    for j in (1, 3, 2):
        zq_copy(j).wait_recv()
        qbuf[FR * j : FR * (j + 1), :] = unpack(qin[j].astype(F32)).astype(BF16)

    ctxt[...] = jnp.zeros_like(ctxt)

    def score_slot(slot, carry):
        top, total = carry
        keys, values = unpack_pair(kvbuf[slot].astype(F32))
        values = values.astype(BF16)
        vbuf[slot] = values
        block = dot(keys.astype(BF16), qbuf[...], NT)
        new_top = jnp.maximum(top, jnp.max(block, axis=0, keepdims=True))
        keep = jnp.exp2((top - new_top) * EXP2_SCALE)
        p = jnp.exp2((block - new_top) * EXP2_SCALE)
        scores[slot] = p
        tops[slot] = new_top
        ctxt[...] = ctxt[...] * keep + dot(values, p.astype(BF16), TN)
        return new_top, total * keep + jnp.sum(p.reshape(FR // 8, 8, QN), axis=0)

    carry = (jnp.full((1, QN), -jnp.inf, F32), jnp.zeros((8, QN), F32))
    carry = lax.fori_loop(0, 4, score_slot, carry)
    for xo in (1, 3, 2):
        for j in (0, 1, 3, 2):
            xkv_copy(xo, j).wait_recv()
            carry = score_slot(xo * 4 + j, carry)
    row_top, total = carry
    inverse = 1.0 / jnp.sum(total, axis=0, keepdims=True)
    wide = ctxt[...] * inverse
    ctxt[...] = wide
    narrow = wide.T
    for j in range(4):
        ctxs[j] = pack(narrow[j * FR : (j + 1) * FR, :]).astype(BF16)

    def ctx_copy(k):
        return copy_to(ctxs.at[k % 4], ctxr.at[k], ctx_s.at[k], ctx_r.at[k], zdev((z - k + 16) % 16))

    for k in order:
        ctx_copy(k).start()
    ctxr[0] = ctxs[0]

    for j in range(4):
        acc = None
        for i in range(4):
            k = j + 4 * i
            if k == 0:
                part = gcs[0]
            else:
                gc_copy(k).wait_recv()
                part = gcr[k]
            part = part.astype(F32)
            acc = part if acc is None else acc + part
        gall[j * FR : (j + 1) * FR, :] = unpack(acc).astype(BF16)
    delta = jnp.sum(gall[...].astype(F32).T * ctxt[...], axis=0, keepdims=True)

    dqt[...] = jnp.zeros_like(dqt)

    def back_slot(slot):
        p = scores[slot] * (jnp.exp2((tops[slot] - row_top) * EXP2_SCALE) * inverse)
        gprob = dot(vbuf[slot], gall[...], NT)
        ds = (p * (gprob - delta) * SCALE).astype(BF16)
        dk = dot(ds, qbuf[...], NN)
        dv = dot(p.astype(BF16), gall[...], NN)
        dqt[...] += dot(kvbuf[slot, 0:160, 0:96], ds, TN)
        return pack_pair(dk, dv)

    def rs_copy(slot):
        xo = slot // 4
        return copy_to(rss.at[slot], rsr.at[slot], rs_s.at[slot], rs_r.at[slot], xdev((x - xo + 4) % 4))

    def away_slot(i, carry):
        slot = 15 - i
        rss[slot] = back_slot(slot).astype(BF16)
        rs_copy(slot).start()
        return carry

    lax.fori_loop(0, 12, away_slot, 0)

    def own_slot(slot, carry):
        own_kv[slot] = back_slot(slot)
        return carry

    lax.fori_loop(0, 4, own_slot, 0)

    dqf[...] = dqt[...].T

    def gq_copy(k):
        return copy_to(gqs.at[k], gqr.at[k], gq_s.at[k], gq_r.at[k], zdev((z - k + 16) % 16))

    def gk_copy(k):
        return copy_to(gks.at[k], gkr.at[k], gk_s.at[k], gk_r.at[k], zdev((z - k + 16) % 16))

    def piece_start(k):
        return pl.multiple_of(40 * (((z - k + 16) % 16) // 4), 8)

    def gq_piece(k):
        return pack(dqf[pl.ds(FR * (k % 4) + piece_start(k), 40), :]).astype(BF16)

    for k in order:
        gqs[k] = gq_piece(k)
        gq_copy(k).start()
    gqr[0] = gq_piece(0)

    for j in range(4):
        for xo in (3, 2, 1):
            rs_copy(xo * 4 + j).wait_recv()
        summed = (
            own_kv[j] + rsr[4 + j].astype(F32) + rsr[8 + j].astype(F32) + rsr[12 + j].astype(F32)
        )
        gk_all[j], gv_all[j] = unpack_pair(summed)

    def gk_piece(k):
        rows40 = pl.ds(piece_start(k), 40)
        return pack(
            jnp.concatenate([gk_all[k % 4, rows40, :], gv_all[k % 4, rows40, :]], axis=0)
        ).astype(BF16)

    for k in order:
        gks[k] = gk_piece(k)
        gk_copy(k).start()
    gkr[0] = gk_piece(0)


    att_acc[...] = jnp.zeros_like(att_acc)

    def owner(k):
        h = (z + k) % 16
        return h // 2, h % 2

    def gp_copy(k):
        dd, hh = owner(k)
        e = (dd - d + 8) % 8
        return copy_to(gps.at[k], gpr.at[e, hh], gp_s.at[k], gp_r.at[e, hh], ddev(dd))

    for k in (0,) + order[::-1]:
        if k > 0:
            ctx_copy(k).wait_recv()
        h = (z + k) % 16
        dd, hh = owner(k)
        context = unpack(ctxr[k].astype(F32)).astype(BF16)
        att_acc[...] += dot(context, w_ref[pl.ds(pl.multiple_of(HD * h, 32), HD), :], NN)
        part = dot(context, go_ref[...], TN)

        @pl.when(dd == d)
        def _():
            gpo[hh] = part

        @pl.when(dd != d)
        def _():
            gps[k] = part.astype(BF16)
            gp_copy(k).start()

    for hh in range(2):
        for e in range(1, 8):
            copy_to(gps.at[0], gpr.at[e, hh], gp_s.at[0], gp_r.at[e, hh], ddev((d + e) % 8)).wait_recv()
        acc = gpo[hh]
        for e in range(1, 8):
            acc = acc + gpr[e, hh].astype(F32)
        gsum[96 * hh : 96 * (hh + 1), :] = acc
        gsb[96 * hh : 96 * (hh + 1), :] = acc.astype(BF16)

    att_ref[...] = att_acc[...].astype(BF16)

    def share(i):
        return pl.ds(pl.multiple_of(16 * i, 16), 16)

    def ps_copy(o):
        i = (s + o) % 16
        return copy_to(gsb.at[share(i)], prr.at[o], ps_s.at[o], ps_r.at[o], {"seq": i})

    def as_copy(o, source):
        rows16 = gpf.at[d, share(source)]
        return copy_to(rows16, rows16, as_s.at[o], as_r.at[o], {"seq": (s + o) % 16})

    for o in range(1, 16):

        @pl.when((s + o) % 16 < 12)
        def _():
            ps_copy(o).start()

    @pl.when(s < 12)
    def _():
        acc = gsum[share(s), :]
        for o in range(1, 16):
            copy_to(gsb.at[0:16], prr.at[o], ps_s.at[o], ps_r.at[o], {"seq": (s + o) % 16}).wait_recv()
            acc = acc + prr[o].astype(F32)
        gpf[d, share(s), :] = acc.astype(BF16)
        for o in range(1, 16):
            as_copy(o, s).start()

    def ad_copy(e, source):
        return copy_to(gpf.at[d], gpf.at[source], ad_s.at[e], ad_r.at[e], ddev((d + 2 * e) % 8))

    def ac_copy(e, mine, other):
        return copy_to(gpf.at[mine], gpf.at[other], ac_s.at[e], ac_r.at[e], ddev(d + 1 - 2 * core))

    def ac_source(e):
        return (d - 2 * e + 8) % 8

    for o in range(1, 16):
        source = (s - o + 16) % 16

        @pl.when(source < 12)
        def _():
            as_copy(o, source).wait_recv()

    for e in (2, 1, 3):
        ad_copy(e, d).start()
    ac_copy(0, d, d).start()

    for k in order:
        gq_copy(k).wait_recv()
        gk_copy(k).wait_recv()

    for group in range(4):
        lanes = pl.ds(CW * group, CW)
        slots = [(4 * group + i - z + 16) % 16 for i in range(4)]
        queries = [unpack(gqr[t].astype(F32)) for t in slots]
        pairs = [unpack(gkr[t].astype(F32)) for t in slots]
        gq_ref[:, lanes] = jnp.concatenate(queries, axis=1).astype(BF16)
        gk_ref[:, lanes] = jnp.concatenate([p[0:40] for p in pairs], axis=1).astype(BF16)
        gv_ref[:, lanes] = jnp.concatenate([p[40:80] for p in pairs], axis=1).astype(BF16)

    for e in (1, 3, 2):
        ad_copy(e, ac_source(e)).wait_recv()
        ac_copy(e, ac_source(e), ac_source(e)).start()
    sibling = d + 1 - 2 * core
    for e in range(4):
        ac_copy(e, d, (sibling - 2 * e + 8) % 8).wait_recv()
    for i in range(8):
        gp_ref[192 * i : 192 * (i + 1), :] = gpf[i]

    for j in range(1, 4):
        zkv_copy(j).wait_send()
        zq_copy(j).wait_send()
    for xo in range(1, 4):
        for j in range(4):
            xkv_copy(xo, j).wait_send()
            rs_copy(xo * 4 + j).wait_send()
    for k in range(1, 16):
        gc_copy(k).wait_send()
        ctx_copy(k).wait_send()
        gq_copy(k).wait_send()
        gk_copy(k).wait_send()
    for k in range(16):

        @pl.when(owner(k)[0] != d)
        def _():
            gp_copy(k).wait_send()

    for o in range(1, 16):

        @pl.when((s + o) % 16 < 12)
        def _():
            ps_copy(o).wait_send()

    @pl.when(s < 12)
    def _():
        for o in range(1, 16):
            as_copy(o, s).wait_send()

    for e in range(1, 4):
        ad_copy(e, d).wait_send()
    for e in range(4):
        ac_copy(e, ac_source(e), ac_source(e)).wait_send()


def per_device(query, key, value, proj_weight, grad_out):
    vmem = pl.BlockSpec(memory_space=pltpu.VMEM)
    dma = pltpu.SemaphoreType.DMA
    width = query.shape[2]
    outs = pl.pallas_call(
        kernel,
        out_shape=(
            jax.ShapeDtypeStruct((FR, CW), BF16),
            jax.ShapeDtypeStruct((40, width), BF16),
            jax.ShapeDtypeStruct((40, width), BF16),
            jax.ShapeDtypeStruct((40, width), BF16),
            jax.ShapeDtypeStruct((width, CW), BF16),
        ),
        in_specs=[pl.BlockSpec(memory_space=pltpu.HBM)] * 5,
        out_specs=(vmem,) * 5,
        scratch_shapes=[
            pltpu.VMEM((FR, width), BF16),
            pltpu.VMEM((FR, width), BF16),
            pltpu.VMEM((FR, width), BF16),
            pltpu.VMEM((width, CW), BF16),
            pltpu.VMEM((FR, CW), BF16),
            pltpu.VMEM((4, 128, 128), BF16),
            pltpu.VMEM((4, 240, 128), BF16),
            pltpu.VMEM((4, 128, 128), BF16),
            pltpu.VMEM((QN, HD), BF16),
            pltpu.VMEM((16, 240, 128), BF16),
            pltpu.VMEM((16, FR, HD), BF16),
            pltpu.VMEM((16, 128, 128), BF16),
            pltpu.VMEM((16, 128, 128), BF16),
            pltpu.VMEM((QN, HD), BF16),
            pltpu.VMEM((16, FR, QN), F32),
            pltpu.VMEM((16, 1, QN), F32),
            pltpu.VMEM((HD, QN), F32),
            pltpu.VMEM((4, 128, 128), BF16),
            pltpu.VMEM((16, 128, 128), BF16),
            pltpu.VMEM((HD, QN), F32),
            pltpu.VMEM((QN, HD), F32),
            pltpu.VMEM((16, 240, 128), BF16),
            pltpu.VMEM((16, 240, 128), BF16),
            pltpu.VMEM((4, 240, 128), F32),
            pltpu.VMEM((4, FR, HD), F32),
            pltpu.VMEM((4, FR, HD), F32),
            pltpu.VMEM((16, 32, 128), BF16),
            pltpu.VMEM((16, 32, 128), BF16),
            pltpu.VMEM((16, 64, 128), BF16),
            pltpu.VMEM((16, 64, 128), BF16),
            pltpu.VMEM((FR, CW), F32),
            pltpu.VMEM((16, HD, CW), BF16),
            pltpu.VMEM((8, 2, HD, CW), BF16),
            pltpu.VMEM((2, HD, CW), F32),
            pltpu.VMEM((192, CW), F32),
            pltpu.VMEM((192, CW), BF16),
            pltpu.VMEM((16, 16, CW), BF16),
            pltpu.VMEM((8, 192, CW), BF16),
            dma((4,)), dma((4,)),
            dma((4,)), dma((4,)),
            dma((16,)), dma((16,)),
            dma((16,)), dma((16,)),
            dma((16,)), dma((16,)),
            dma((16,)), dma((16,)),
            dma((16,)), dma((16,)),
            dma((16,)), dma((16,)),
            dma((16,)), dma((8, 2)),
            dma((16,)), dma((16,)),
            dma((16,)), dma((16,)),
            dma((4,)), dma((4,)),
            dma((4,)), dma((4,)),
            dma((5,)),
        ],
        compiler_params=pltpu.CompilerParams(
            collective_id=0, has_side_effects=True, vmem_limit_bytes=64 * 1024 * 1024 - 65536
        ),
        name="attention",
    )(query[0], key[0], value[0], proj_weight, grad_out[0])
    att, gq, gk, gv, gp = outs
    return att[None], gq[None], gk[None], gv[None], gp


def solution(mesh):
    return jax.shard_map(
        per_device,
        mesh=mesh,
        in_specs=(
            P("dp", "seq", None),
            P("dp", "seq", None),
            P("dp", "seq", None),
            P(None, "mp"),
            P("dp", "seq", "mp"),
        ),
        out_specs=(
            P("dp", "seq", "mp"),
            P("dp", ("seq", "mp"), None),
            P("dp", ("seq", "mp"), None),
            P("dp", ("seq", "mp"), None),
            P(None, "mp"),
        ),
        check_vma=False,
    )
```

time: 141 us -> 119 us (0.84)
  Pallas kernels: 131 us -> 109 us
    pallas_call x1, Pallas kernels: 131 us -> 109 us  [per_device(): pl.pallas_call(kernel, out_shape=(jax.ShapeDtypeStruct((FR, CW), BF16), j...]
    unnamed x15 -> x5, local copies, waits for them, and re-layouts: 8.86 us -> 8.63 us
where the time goes in v2:
time: 119 us; the launch traced here: 118 us
  Pallas kernels  109 us (92%)
  local copies, waits for them, and re-layouts  8.63 us (7%)
    pallas_call x1, Pallas kernels, per_device(): pl.pallas_call(kernel, out_shape=(jax.ShapeDtypeStruct((FR, CW), BF16), j...  109 us
    unnamed x5, local copies, waits for them, and re-layouts  8.63 us

profile of v2, /device:TPU:1, one launch (start us, length us, event | category | flops | bytes accessed | tf_op | source)
XLA Modules:
  0.0 118.3 jit_solution(5097334215507860389)
XLA Ops:
  0.6 109.0 %attention.1 = (bf16[160,384]{1,0:T(8,128)(2,1)}, bf16[40,1536]{1,0:T(8,128)(2,1)}, bf16[40,1536]{1,0:T(8,128)(2,1)}, bf16[40,1536]{1,0:T(8,128)(2,1)}, bf16[1536,384]{1,0:T(8,128)(2,1)}) custom-call(bf16[160,1536]{1,0:T(8,128)(2,1)} %bitcast.8, bf16[160,1536]{1,0:T(8,128)(2,1)} %bitcast.9, bf16[160,1536]{1,0:T(8,128)(2,1)} %bitcast.10, ...), custom_call_target="tpu_custom_call" | custom-call | tf_op jit(solution)/shard_map/attention/pallas_call | solution.py:460
  109.7 1.6 %copy.15 = bf16[1,160,384]{2,1,0:T(8,128)(2,1)} copy(bf16[1,160,384]{2,1,0:T(8,128)(2,1)} %bitcast.15) | data formatting | bytes 245760
  111.2 1.6 %copy.16 = bf16[1,40,1536]{2,1,0:T(8,128)(2,1)} copy(bf16[1,40,1536]{2,1,0:T(8,128)(2,1)} %bitcast.14) | data formatting | bytes 245760
  112.8 1.6 %copy.17 = bf16[1,40,1536]{2,1,0:T(8,128)(2,1)} copy(bf16[1,40,1536]{2,1,0:T(8,128)(2,1)} %bitcast.13) | data formatting | bytes 245760
  114.3 1.6 %copy.18 = bf16[1,40,1536]{2,1,0:T(8,128)(2,1)} copy(bf16[1,40,1536]{2,1,0:T(8,128)(2,1)} %bitcast.12) | data formatting | bytes 245760
  115.9 2.4 %copy.19 = bf16[1536,384]{1,0:T(8,128)(2,1)} copy(bf16[1536,384]{1,0:T(8,128)(2,1)} %get-tuple-element.24) | data formatting | bytes 2359296

commit v3 on v2

--- a/solution.py
+++ b/solution.py
@@ -61,7 +61,7 @@
     q_hbm, k_hbm, v_hbm, w_hbm, go_hbm,
     att_ref, gq_ref, gk_ref, gv_ref, gp_ref,
     q_ref, k_ref, v_ref, w_ref, go_ref,
-    zsq, zskv, qin, qbuf, kvbuf, vbuf, gcs, gcr, gall, scores, tops, ctxt, ctxs, ctxr, dqt, dqf, rss, rsr, own_kv, gk_all, gv_all,
+    zsq, zskv, qin, qbuf, kvbuf, vbuf, gcs, gcm, gcr, gall, scores, tops, ctxt, ctxs, ctxr, dqt, dqf, rss, rsr, own_kv, gk_all, gv_all,
     gqs, gqr, gks, gkr, att_acc, gps, gpr, gpo, gsum, gsb, prr, gpf,
     zq_s, zq_r, zkv_s, zkv_r, xkv_s, xkv_r, gc_s, gc_r, ctx_s, ctx_r, rs_s, rs_r,
     gq_s, gq_r, gk_s, gk_r, gp_s, gp_r, ps_s, ps_r, as_s, as_r, ad_s, ad_r, ac_s, ac_r, in_s,
@@ -168,7 +168,17 @@
     fetches[4].wait()
 
     def gc_copy(k):
+        if 5 <= k <= 11:
+            step = 4 if k <= 8 else -4
+            return copy_to(gcs.at[k], gcm.at[k], gc_s.at[k], gc_r.at[k], zdev((z + step + 16) % 16))
         return copy_to(gcs.at[k], gcr.at[k], gc_s.at[k], gc_r.at[k], zdev((z + k) % 16))
+
+    def gc_relay():
+        for k in (4, 3, 13, 2, 14, 1, 15):
+            far = k + 4 if k < 8 else k - 4
+            gc_copy(far).wait_recv()
+            gcs[k] = (gcs[k].astype(F32) + gcm[far].astype(F32)).astype(BF16)
+            gc_copy(k).start()
 
     def gc_step(k):
         h = (z + k) % 16
@@ -176,14 +186,18 @@
         gcs[k] = pack(part).astype(BF16)
 
     order = (8, 7, 9, 6, 10, 5, 11, 4, 12, 3, 13, 2, 14, 1, 15)
-    for k in order:
+    for k in order[:5]:
         gc_step(k)
     for j in (1, 3, 2):
         zkv_copy(j).wait_recv()
         for xo in (2, 1, 3):
             xkv_copy(xo, j).start()
-    for k in order:
+    for k in order[:5]:
         gc_copy(k).start()
+    for k in order[5:]:
+        gc_step(k)
+        if 5 <= k <= 12:
+            gc_copy(k).start()
     gcs[0] = pack(dot(go_ref[...], w_ref[pl.ds(pl.multiple_of(HD * z, 32), HD), :], NT)).astype(BF16)
 
     for j in (1, 3, 2):
@@ -212,6 +226,8 @@
         for j in (0, 1, 3, 2):
             xkv_copy(xo, j).wait_recv()
             carry = score_slot(xo * 4 + j, carry)
+        if xo == 1:
+            gc_relay()
     row_top, total = carry
     inverse = 1.0 / jnp.sum(total, axis=0, keepdims=True)
     wide = ctxt[...] * inverse
@@ -221,25 +237,56 @@
         ctxs[j] = pack(narrow[j * FR : (j + 1) * FR, :]).astype(BF16)
 
     def ctx_copy(k):
-        return copy_to(ctxs.at[k % 4], ctxr.at[k], ctx_s.at[k], ctx_r.at[k], zdev((z - k + 16) % 16))
-
-    for k in order:
+        if 5 <= k <= 11:
+            source, step = (ctxr.at[k - 4], -4) if k <= 8 else (ctxr.at[k + 4], 4)
+        else:
+            source, step = ctxs.at[k % 4], -k
+        return copy_to(source, ctxr.at[k], ctx_s.at[k], ctx_r.at[k], zdev((z + step + 16) % 16))
+
+    for k in (4, 12, 3, 13, 2, 14, 1, 15):
         ctx_copy(k).start()
     ctxr[0] = ctxs[0]
 
     for j in range(4):
-        acc = None
-        for i in range(4):
-            k = j + 4 * i
-            if k == 0:
-                part = gcs[0]
-            else:
-                gc_copy(k).wait_recv()
-                part = gcr[k]
-            part = part.astype(F32)
+        acc = gcs[0].astype(F32) if j == 0 else None
+        for k in (4, 12) if j == 0 else (j, j + 12):
+            gc_copy(k).wait_recv()
+            part = gcr[k].astype(F32)
             acc = part if acc is None else acc + part
         gall[j * FR : (j + 1) * FR, :] = unpack(acc).astype(BF16)
+    for k in (4, 3, 13, 2, 14, 1, 15):
+        ctx_copy(k).wait_recv()
+        ctx_copy(k + 4 if k < 8 else k - 4).start()
     delta = jnp.sum(gall[...].astype(F32).T * ctxt[...], axis=0, keepdims=True)
+
+    att_acc[...] = jnp.zeros_like(att_acc)
+
+    def owner(k):
+        h = (z + k) % 16
+        return h // 2, h % 2
+
+    def gp_copy(k):
+        dd, hh = owner(k)
+        e = (dd - d + 8) % 8
+        return copy_to(gps.at[k], gpr.at[e, hh], gp_s.at[k], gp_r.at[e, hh], ddev(dd))
+
+    def project(k):
+        if 5 <= k <= 12:
+            ctx_copy(k).wait_recv()
+        h = (z + k) % 16
+        dd, hh = owner(k)
+        context = unpack(ctxr[k].astype(F32)).astype(BF16)
+        att_acc[...] += dot(context, w_ref[pl.ds(pl.multiple_of(HD * h, 32), HD), :], NN)
+        part = dot(context, go_ref[...], TN)
+
+        @pl.when(dd == d)
+        def _():
+            gpo[hh] = part
+
+        @pl.when(dd != d)
+        def _():
+            gps[k] = part.astype(BF16)
+            gp_copy(k).start()
 
     dqt[...] = jnp.zeros_like(dqt)
 
@@ -263,6 +310,9 @@
         return carry
 
     lax.fori_loop(0, 12, away_slot, 0)
+    project(0)
+    for k in order[:8:-1]:
+        project(k)
 
     def own_slot(slot, carry):
         own_kv[slot] = back_slot(slot)
@@ -288,6 +338,9 @@
         gqs[k] = gq_piece(k)
         gq_copy(k).start()
     gqr[0] = gq_piece(0)
+
+    for k in order[8:3:-1]:
+        project(k)
 
     for j in range(4):
         for xo in (3, 2, 1):
@@ -309,34 +362,8 @@
     gkr[0] = gk_piece(0)
 
 
-    att_acc[...] = jnp.zeros_like(att_acc)
-
-    def owner(k):
-        h = (z + k) % 16
-        return h // 2, h % 2
-
-    def gp_copy(k):
-        dd, hh = owner(k)
-        e = (dd - d + 8) % 8
-        return copy_to(gps.at[k], gpr.at[e, hh], gp_s.at[k], gp_r.at[e, hh], ddev(dd))
-
-    for k in (0,) + order[::-1]:
-        if k > 0:
-            ctx_copy(k).wait_recv()
-        h = (z + k) % 16
-        dd, hh = owner(k)
-        context = unpack(ctxr[k].astype(F32)).astype(BF16)
-        att_acc[...] += dot(context, w_ref[pl.ds(pl.multiple_of(HD * h, 32), HD), :], NN)
-        part = dot(context, go_ref[...], TN)
-
-        @pl.when(dd == d)
-        def _():
-            gpo[hh] = part
-
-        @pl.when(dd != d)
-        def _():
-            gps[k] = part.astype(BF16)
-            gp_copy(k).start()
+    for k in order[3::-1]:
+        project(k)
 
     for hh in range(2):
         for e in range(1, 8):
@@ -482,6 +509,7 @@
             pltpu.VMEM((16, FR, HD), BF16),
             pltpu.VMEM((16, 128, 128), BF16),
             pltpu.VMEM((16, 128, 128), BF16),
+            pltpu.VMEM((16, 128, 128), BF16),
             pltpu.VMEM((QN, HD), BF16),
             pltpu.VMEM((16, FR, QN), F32),
             pltpu.VMEM((16, 1, QN), F32),

time: 119 us -> 114 us (0.958)
  Pallas kernels: 109 us -> 105 us
    pallas_call x1, Pallas kernels: 109 us -> 105 us  [per_device(): pl.pallas_call(kernel, out_shape=(jax.ShapeDtypeStruct((FR, CW), BF16), j...]
where the time goes in v3:
time: 114 us
  Pallas kernels  105 us (92%)
  local copies, waits for them, and re-layouts  8.63 us (8%)
    pallas_call x1, Pallas kernels, per_device(): pl.pallas_call(kernel, out_shape=(jax.ShapeDtypeStruct((FR, CW), BF16), j...  105 us
    unnamed x5, local copies, waits for them, and re-layouts  8.63 us

profile of v3, /device:TPU:1, one launch (start us, length us, event | category | flops | bytes accessed | tf_op | source)
XLA Modules:
  0.0 113.8 jit_solution(3013692162592982537)
XLA Ops:
  0.6 104.5 %attention.1 = (bf16[160,384]{1,0:T(8,128)(2,1)}, bf16[40,1536]{1,0:T(8,128)(2,1)}, bf16[40,1536]{1,0:T(8,128)(2,1)}, bf16[40,1536]{1,0:T(8,128)(2,1)}, bf16[1536,384]{1,0:T(8,128)(2,1)}) custom-call(bf16[160,1536]{1,0:T(8,128)(2,1)} %bitcast.8, bf16[160,1536]{1,0:T(8,128)(2,1)} %bitcast.9, bf16[160,1536]{1,0:T(8,128)(2,1)} %bitcast.10, ...), custom_call_target="tpu_custom_call" | custom-call | tf_op jit(solution)/shard_map/attention/pallas_call | solution.py:487
  105.2 1.6 %copy.15 = bf16[1,160,384]{2,1,0:T(8,128)(2,1)} copy(bf16[1,160,384]{2,1,0:T(8,128)(2,1)} %bitcast.15) | data formatting | bytes 245760
  106.7 1.6 %copy.16 = bf16[1,40,1536]{2,1,0:T(8,128)(2,1)} copy(bf16[1,40,1536]{2,1,0:T(8,128)(2,1)} %bitcast.14) | data formatting | bytes 245760
  108.3 1.6 %copy.17 = bf16[1,40,1536]{2,1,0:T(8,128)(2,1)} copy(bf16[1,40,1536]{2,1,0:T(8,128)(2,1)} %bitcast.13) | data formatting | bytes 245760
  109.8 1.6 %copy.18 = bf16[1,40,1536]{2,1,0:T(8,128)(2,1)} copy(bf16[1,40,1536]{2,1,0:T(8,128)(2,1)} %bitcast.12) | data formatting | bytes 245760
  111.4 2.4 %copy.19 = bf16[1536,384]{1,0:T(8,128)(2,1)} copy(bf16[1536,384]{1,0:T(8,128)(2,1)} %get-tuple-element.24) | data formatting | bytes 2359296

commit v4 on v3

--- a/solution.py
+++ b/solution.py
@@ -311,7 +311,7 @@
 
     lax.fori_loop(0, 12, away_slot, 0)
     project(0)
-    for k in order[:8:-1]:
+    for k in (15, 1, 14, 2, 13, 3):
         project(k)
 
     def own_slot(slot, carry):
@@ -339,7 +339,7 @@
         gq_copy(k).start()
     gqr[0] = gq_piece(0)
 
-    for k in order[8:3:-1]:
+    for k in (12, 4, 8, 7, 9):
         project(k)
 
     for j in range(4):
@@ -362,7 +362,7 @@
     gkr[0] = gk_piece(0)
 
 
-    for k in order[3::-1]:
+    for k in (6, 10, 5, 11):
         project(k)
 
     for hh in range(2):

time: 114 us -> 114 us (level)
  no operation moved by 1% of the time
where the time goes in v4:
time: 114 us; the launch traced here: 113 us
  Pallas kernels  104 us (91%)
  local copies, waits for them, and re-layouts  8.63 us (8%)
    pallas_call x1, Pallas kernels, per_device(): pl.pallas_call(kernel, out_shape=(jax.ShapeDtypeStruct((FR, CW), BF16), j...  104 us
    unnamed x5, local copies, waits for them, and re-layouts  8.63 us

profile of v4, /device:TPU:1, one launch (start us, length us, event | category | flops | bytes accessed | tf_op | source)
XLA Modules:
  0.0 113.5 jit_solution(2551116303606701127)
XLA Ops:
  0.6 104.2 %attention.1 = (bf16[160,384]{1,0:T(8,128)(2,1)}, bf16[40,1536]{1,0:T(8,128)(2,1)}, bf16[40,1536]{1,0:T(8,128)(2,1)}, bf16[40,1536]{1,0:T(8,128)(2,1)}, bf16[1536,384]{1,0:T(8,128)(2,1)}) custom-call(bf16[160,1536]{1,0:T(8,128)(2,1)} %bitcast.8, bf16[160,1536]{1,0:T(8,128)(2,1)} %bitcast.9, bf16[160,1536]{1,0:T(8,128)(2,1)} %bitcast.10, ...), custom_call_target="tpu_custom_call" | custom-call | tf_op jit(solution)/shard_map/attention/pallas_call | solution.py:487
  104.9 1.6 %copy.15 = bf16[1,160,384]{2,1,0:T(8,128)(2,1)} copy(bf16[1,160,384]{2,1,0:T(8,128)(2,1)} %bitcast.15) | data formatting | bytes 245760
  106.4 1.6 %copy.16 = bf16[1,40,1536]{2,1,0:T(8,128)(2,1)} copy(bf16[1,40,1536]{2,1,0:T(8,128)(2,1)} %bitcast.14) | data formatting | bytes 245760
  108.0 1.6 %copy.17 = bf16[1,40,1536]{2,1,0:T(8,128)(2,1)} copy(bf16[1,40,1536]{2,1,0:T(8,128)(2,1)} %bitcast.13) | data formatting | bytes 245760
  109.5 1.6 %copy.18 = bf16[1,40,1536]{2,1,0:T(8,128)(2,1)} copy(bf16[1,40,1536]{2,1,0:T(8,128)(2,1)} %bitcast.12) | data formatting | bytes 245760
  111.1 2.4 %copy.19 = bf16[1536,384]{1,0:T(8,128)(2,1)} copy(bf16[1536,384]{1,0:T(8,128)(2,1)} %get-tuple-element.24) | data formatting | bytes 2359296
